TPU v7x, 128 devices: a whole 4x4x4 slice. The times are simulated.
128 devices in a mesh: dp: 8 (over x_hi, y), tm: 8 (over z, core), height: 2 (over x_lo).
Axes of the slice: x: 4 (x_hi: 2, x_lo: 2; x = x_hi * 2 + x_lo), y: 4, z: 4, core: 2. Of those that a mesh axis runs over, the one named last changes fastest.
Arguments:
- block_input: bfloat16 [8, 16, 16, 64, 384], P('dp', 'tm', 'height'), may hold values from -6 to 6
- block_output: bfloat16 [8, 16, 16, 64, 384], P('dp', None, 'height', 'tm'), may hold values from -6 to 6
- latent_grad: float32 [8, 16, 16, 1024], P('dp', None, 'height', 'tm'), may hold values from -6 to 6
- seeds: int32 [8], P('dp'), may hold values from 0 to 29999
- lengths: int32 [8], P('dp'), may hold values from 1 to 16, as said below
- conv_weight: bfloat16 [384, 27, 384], P(('dp', 'tm', 'height')), may hold values from -0.0625 to 0.0625
- head_weight: bfloat16 [384, 32], replicated, may hold values from -0.3125 to 0.3125
Outputs:
- input_grad: bfloat16 [8, 16, 16, 64, 384], P('dp', 'tm', 'height')
- conv_grad: float32 [384, 27, 384], P(('dp', 'tm', 'height'))
- head_grad: float32 [384, 32], P(('dp', 'tm', 'height'))
Inputs may be any that keep to these rules, and one draw needn't show every extreme that they name: `lengths`: some clip has all 16 frames valid in every draw.
All inputs are finite; a program needn't handle non-finite values.
Results may differ from a plain program's by a relative error of at most 0.0075.
Values may be sent and summed in bfloat16 or wider, within the bound.
A program may use at most 192 MiB of HBM per device.

v0:
```python
import math

import jax
import jax.numpy as jnp
from jax import lax
from jax.sharding import PartitionSpec as P

EPSILON = 1e-06
ROOT_THREE = math.sqrt(3.0)
OFFSETS = [
    (frame_off, row_off, col_off)
    for frame_off in range(3)
    for row_off in range(3)
    for col_off in range(3)
]


def padded(cells, sides, width):
    for axis, dim in sides:
        count = lax.axis_size(axis)
        ends = count - 1
        head = lax.slice_in_dim(cells, 0, width, axis=dim)
        tail = lax.slice_in_dim(cells, cells.shape[dim] - width, cells.shape[dim], axis=dim)
        cells = jnp.concatenate(
            [
                lax.ppermute(tail, axis, [(i, (i + 1) % count) for i in range(ends)]),
                cells,
                lax.ppermute(head, axis, [((i + 1) % count, i) for i in range(ends)]),
            ],
            axis=dim,
        )
    return cells


def silu_slope(values):
    logistic = jax.nn.sigmoid(values)
    return logistic * (1.0 + values * (1.0 - logistic))


def norm_back(grad_in, normed, inverse):
    return inverse * (grad_in - normed * jnp.mean(grad_in * normed, axis=-1, keepdims=True))


def unit_noise(seed_value, position):
    primary = (seed_value * 7919 + position) % 30269
    primary = (primary * primary + 7) % 30269
    primary = (primary * primary + 101) % 30269
    secondary = (seed_value * 7907 + position * 3) % 30307
    secondary = (secondary * secondary + 13) % 30307
    secondary = (secondary * secondary + 211) % 30307
    combined = (primary + secondary) % 30269
    return ROOT_THREE * ((combined.astype(jnp.float32) + 0.5) * (2.0 / 30269.0) - 1.0)


def per_device(block_input, block_output, latent_grad, seeds, lengths, conv_weight, head_weight):
    tile_input = lax.all_to_all(block_input, "tm", split_axis=3, concat_axis=1, tiled=True)[0]
    frames, tile_rows, tile_cols, channels = tile_input.shape
    cell_count = frames * tile_rows * tile_cols
    latent_dim = head_weight.shape[1] // 2
    total_rows = tile_rows * lax.axis_size("height")
    total_cols = tile_cols * lax.axis_size("tm")
    scaling = 1.0 / math.sqrt(lax.axis_size("dp") * frames * total_rows * total_cols)
    input_f = tile_input.astype(jnp.float32)
    inverse_in = lax.rsqrt(jnp.mean(input_f * input_f, axis=-1, keepdims=True) + EPSILON)
    normed_in = input_f * inverse_in
    active = jax.nn.silu(normed_in).astype(jnp.bfloat16)
    rimmed = padded(active, (("tm", 2), ("height", 1)), 1)
    padded_act = jnp.pad(rimmed, ((2, 0), (0, 0), (0, 0), (0, 0)))
    output_f = block_output[0].astype(jnp.float32).reshape(cell_count, channels)
    inverse_out = lax.rsqrt(jnp.mean(output_f * output_f, axis=-1, keepdims=True) + EPSILON)
    normed_out = output_f * inverse_out
    active_out = jax.nn.silu(normed_out).astype(jnp.bfloat16)
    latent = jnp.dot(active_out, head_weight, preferred_element_type=jnp.float32)
    mean_part = latent[:, :latent_dim]
    logvar = latent[:, latent_dim:]
    frame_ids = jnp.arange(frames, dtype=jnp.int32)[:, None, None, None]
    row_ids = (lax.axis_index("height") * tile_rows + jnp.arange(tile_rows, dtype=jnp.int32))[
        None, :, None, None
    ]
    col_ids = (lax.axis_index("tm") * tile_cols + jnp.arange(tile_cols, dtype=jnp.int32))[
        None, None, :, None
    ]
    chan_ids = jnp.arange(latent_dim, dtype=jnp.int32)[None, None, None, :]
    position = (
        ((frame_ids * total_rows + row_ids) * total_cols + col_ids) * latent_dim + chan_ids
    ).reshape(cell_count, latent_dim)
    noise = unit_noise(seeds[0], position)
    frame_valid = jnp.broadcast_to(
        (jnp.arange(frames, dtype=jnp.int32) < lengths[0])[:, None, None, None],
        (frames, tile_rows, tile_cols, 1),
    )
    frame_valid = frame_valid.reshape(cell_count, 1).astype(jnp.float32)
    upstream = latent_grad[0].reshape(cell_count, latent_dim)
    grad_mean = frame_valid * (upstream + mean_part)
    grad_logvar = frame_valid * (
        0.5 * upstream * noise * jnp.exp(0.5 * logvar) + 0.5 * (jnp.exp(logvar) - 1.0)
    )
    head_in = jnp.concatenate([grad_mean, grad_logvar], axis=1).astype(jnp.bfloat16)
    grad_active = lax.dot_general(
        head_in, head_weight, (((1,), (1,)), ((), ())), preferred_element_type=jnp.float32
    )
    grad_sum = norm_back(grad_active * silu_slope(normed_out), normed_out, inverse_out)
    grad_conv = grad_sum.astype(jnp.bfloat16)
    row_count = (
        channels // lax.axis_size(("dp", "tm", "height")) * lax.axis_size(("dp", "tm", "height"))
    )
    pieces = []
    for offset in OFFSETS:
        window = lax.dynamic_slice(
            padded_act,
            (offset[0], offset[1], offset[2], 0),
            (frames, tile_rows, tile_cols, row_count),
        )
        window = window.reshape(cell_count, row_count)
        pieces.append(
            lax.dot_general(
                window, grad_conv, (((0,), (0,)), ((), ())), preferred_element_type=jnp.float32
            )
        )
    conv_part = jnp.stack(pieces, axis=1).reshape(row_count, 27 * channels)
    head_part = lax.dot_general(
        active_out, head_in, (((0,), (0,)), ((), ())), preferred_element_type=jnp.float32
    )
    summed = lax.psum_scatter(
        jnp.concatenate([conv_part, head_part], axis=1) * scaling,
        ("dp", "tm", "height"),
        scatter_dimension=0,
        tiled=True,
    )
    conv_grad = summed[:, : 27 * channels].reshape(summed.shape[0], 27, channels)
    head_grad = summed[:, 27 * channels :]
    grad_rimmed = padded(
        grad_conv.reshape(frames, tile_rows, tile_cols, channels), (("tm", 2), ("height", 1)), 1
    )
    padded_grad = jnp.pad(grad_rimmed, ((0, 2), (0, 0), (0, 0), (0, 0)))
    weight_piece = lax.all_gather(conv_weight, ("dp", "tm", "height"), axis=0, tiled=True)
    accumulated = jnp.zeros((cell_count, weight_piece.shape[0]), jnp.float32)
    for number, offset in enumerate(OFFSETS):
        back_window = padded_grad[
            2 - offset[0] : 2 - offset[0] + frames,
            2 - offset[1] : 2 - offset[1] + tile_rows,
            2 - offset[2] : 2 - offset[2] + tile_cols,
        ]
        back_window = back_window.reshape(cell_count, channels)
        accumulated = accumulated + lax.dot_general(
            back_window,
            weight_piece[:, number, :],
            (((1,), (1,)), ((), ())),
            preferred_element_type=jnp.float32,
        )
    normed_flat = normed_in.reshape(cell_count, channels)
    inverse_flat = inverse_in.reshape(cell_count, 1)
    input_grad = grad_sum + norm_back(
        accumulated * silu_slope(normed_flat), normed_flat, inverse_flat
    )
    input_grad = input_grad.astype(jnp.bfloat16).reshape(1, frames, tile_rows, tile_cols, channels)
    input_grad = lax.all_to_all(input_grad, "tm", split_axis=1, concat_axis=3, tiled=True)
    return (input_grad, conv_grad, head_grad)


def solution(mesh):
    placed = (
        P("dp", "tm", "height", None, None),
        P("dp", None, "height", "tm", None),
        P("dp", None, "height", "tm"),
        P("dp"),
        P("dp"),
        P(("dp", "tm", "height"), None, None),
        P(),
    )
    return jax.shard_map(
        per_device,
        mesh=mesh,
        in_specs=placed,
        out_specs=(
            P("dp", "tm", "height", None, None),
            P(("dp", "tm", "height"), None, None),
            P(("dp", "tm", "height"), None),
        ),
        check_vma=False,
    )
```

profile of v0, /device:TPU:1, one launch (start us, length us, event | category | flops | bytes accessed | tf_op | source)
XLA Modules:
  0.0 687.2 jit_solution(2068932248777137985)
XLA Ops:
  7.9 2.5 copy.107
  10.5 6.9 %all-to-all-start = ((bf16[1,2,8,64,384]{4,2,1,0,3:T(8,128)(2,1)}), bf16[1,2,8,64,384]{4,2,1,0,3:T(8,128)(2,1)S(1)}, u32[]{:S(2)}, u32[]{:S(2)}) async-start(bf16[1,2,8,64,384]{4,2,1,0,3:T(8,128)(2,1)} %copy.107), calls=%async_computation | async-start | bytes 1572864 | tf_op jit(solution)/shard_map/all_to_all | solution.py:56
  23.9 2.0 collective-permute-start.1
  25.9 3.6 collective-permute-start
  33.7 4.2 collective-permute-start.2
  37.9 1.9 pad_maximum_fusion.5
  41.3 2.4 pad_maximum_fusion
  43.7 2.3 fusion.11
  46.0 2.8 fusion.113
  48.8 5.7 fusion.110
  58.1 1.9 collective-permute-start.5
  60.0 5.2 collective-permute-start.4
  69.6 4.0 collective-permute-start.6
  73.7 1.9 pad_maximum_fusion.2
  77.2 2.5 fusion.15
  79.7 4.2 fusion.109
  84.0 2.7 fusion.44
  111.3 2.8 pad_maximum_fusion.1
  114.0 2.1 fusion.111
  122.0 208.6 %all-gather.2.cloned.1.call-done = bf16[384,27,384]{2,1,0:T(8,128)(2,1)} async-done(((bf16[3,27,384]{2,1,0:T(8,128)(2,1)}), bf16[384,27,384]{2,1,0:T(8,128)(2,1)}) %all-gather.2.cloned.1.call-update) | async-done | bytes 7962640 | tf_op jit(solution)/shard_map/all_gather | solution.py:136
  330.6 23.8 %fusion.107 = (bf16[384,1,384]{2,1,0:T(2,128)(2,1)}, bf16[384,1,384]{2,1,0:T(2,128)(2,1)S(1)}, bf16[384,1,384]{2,1,0:T(2,128)(2,1)S(1)}, bf16[384,1,384]{2,1,0:T...) fusion(bf16[384,27,384]{2,1,0:T(8,128)(2,1)} %all-gather.2.clon, ...), kind=kLoop, calls=%fused_computation.218 | loop fusion | bytes 11206656 | tf_op jit(solution)/shard_map/slice | solution.py:147
  357.3 1.8 fusion.47
  359.1 1.8 fusion.48
  360.9 1.8 fusion.50
  362.7 1.9 fusion.51
  364.6 1.8 fusion.52
  366.4 1.8 fusion.53
  368.2 1.9 fusion.54
  370.1 1.9 fusion.55
  372.0 1.8 fusion.56
  373.7 1.8 fusion.57
  377.4 1.8 fusion.59
  382.8 1.8 fusion.62
  386.4 4.5 fusion.108
  391.0 1.8 fusion.64
  394.6 1.8 fusion.66
  396.4 1.8 fusion.67
  398.3 1.8 fusion.68
  400.1 1.9 fusion.69
  403.8 1.8 fusion.70
  405.6 16.4 %multiply_convert_fusion = (bf16[1024,384]{1,0:T(8,128)(2,1)}, f32[1024]{0:T(1024)S(1)}, f32[1024,384]{1,0:T(8,128)}) fusion(f32[1,2,8,8,8,384]{5,4,2,1,3,0:T(8,128)S(1)} %copy.137, f32[1024]{0:T(1024)S(1)} %rsqrt.34, f32[1024,384]{1,0:T(8,128)S(1)} %copy-done.5, bf16[1024,384]{1,0:T(8,128)(2,1)} %bitcast.437, bf16[384,1,384]{2,1,0:T(2,128)(2,1)} %get-tuple-element.3, ...), kind=kOutput, calls=%fused_computation.28 | convolution fusion | flops 318503936 | bytes 47489024 | tf_op jit(solution)/shard_map/dot_general | solution.py:145
  422.0 2.6 fusion.22
  430.5 16.5 %copy.141 = f32[384,10368]{1,0:T(8,128)} copy(f32[384,10368]{0,1:T(8,128)} %bitcast.122) | data formatting | bytes 31850496 | tf_op jit(solution)/shard_map/reshape | solution.py:120
  446.9 11.2 %maximum_multiply_fusion = f32[384,10400]{1,0:T(8,128)} fusion(f32[384,32]{1,0:T(8,128)S(1)} %copy-done.40, f32[384,10368]{1,0:T(8,128)} %copy.141), kind=kLoop, calls=%fused_computation | loop fusion | flops 7987200 | bytes 31948800 | tf_op jit(solution)/shard_map/mul | solution.py:125
  458.2 3.1 add_convert_fusion
  461.2 4.4 all-to-all-start.1
  465.6 16.2 %all-to-all-done.1 = bf16[1,16,8,8,384]{4,3,2,0,1:T(8,128)(2,1)S(1)} async-done(((bf16[1,16,8,8,384]{4,3,2,0,1:T(8,128)(2,1)}), bf16[1,16,8,8,384]{4,3,2,0,1:T(8,128)(2,1)S(1)}, u32[]{:S(2)}, u32[]{:S(2)}) %all-to-all-start.1) | async-done | bytes 786464 | tf_op jit(solution)/shard_map/all_to_all | solution.py:157
  482.9 194.1 %all-reduce.5.cloned.1.call-done = f32[384,10400]{1,0:T(8,128)} async-done(((f32[384,10400]{1,0:T(8,128)}), f32[384,10400]{1,0:T(8,128)}) %all-reduce.5.cloned.1.call-update) | async-done | bytes 15974416
  (186 shorter events, 75.2 us)
Async XLA Ops:
  7.2 13.3 %copy-start = (bf16[384,32]{0,1:T(8,128)(2,1)S(1)}, bf16[384,32]{0,1:T(8,128)(2,1)}, u32[]{:S(2)}) copy-start(bf16[384,32]{0,1:T(8,128)(2,1)} %param.13) | copy-start | bytes 73732
  7.2 323.4 %all-gather.2.cloned.1.call-start = ((), (), s32[]{:S(2)}) async-start(), calls=%async_computation.2 | async-start | bytes 9510912 | tf_op jit(solution)/shard_map/all_gather | solution.py:136
  7.9 9.5 %copy-start.2 = (bf16[1,16,8,8,384]{4,3,2,1,0:T(8,128)(2,1)S(1)}, bf16[1,16,8,8,384]{4,3,2,1,0:T(8,128)(2,1)}, u32[]{:S(2)}) copy-start(bf16[1,16,8,8,384]{4,3,2,1,0:T(8,128)(2,1)} %param.8) | copy-start | bytes 2359300
  10.5 7.3 %copy-start.45 = (f32[1,16,8,128]{3,2,1,0:T(8,128)S(1)}, f32[1,16,8,128]{3,2,1,0:T(8,128)}, u32[]{:S(2)}) copy-start(f32[1,16,8,128]{3,2,1,0:T(8,128)} %param.9) | copy-start | bytes 196612
  10.5 44.0 %all-to-all-start = ((bf16[1,2,8,64,384]{4,2,1,0,3:T(8,128)(2,1)}), bf16[1,2,8,64,384]{4,2,1,0,3:T(8,128)(2,1)S(1)}, u32[]{:S(2)}, u32[]{:S(2)}) async-start(bf16[1,2,8,64,384]{4,2,1,0,3:T(8,128)(2,1)} %copy.107), calls=%async_computation | async-start | bytes 1572864 | tf_op jit(solution)/shard_map/all_to_all | solution.py:56
  17.4 659.5 %all-reduce.5.cloned.1.call-start = ((), (), s32[]{:S(2)}) async-start(), calls=%async_computation.3 | async-start | bytes 32243712
  23.9 7.9 %collective-permute-start.1 = (bf16[16,8,1,384]{3,2,1,0:T(2,128)(2,1)S(1)}, bf16[16,8,1,384]{3,2,1,0:T(2,128)(2,1)S(1)}, u32[]{:S(2)}, u32[]{:S(2)}) collective-permute-start(bf16[16,8,1,384]{3,2,1,0:T(2,128)(2,1)S(1)} %get-tuple-element.97), channel_id=1, source_target_pairs={{2,0},{4,2},{6,4},{8,6},{10,8},{12,10},{14,12},{3,1},{5,3},{7,5},{... | collective-permute-start | bytes 294920 | tf_op jit(solution)/shard_map/ppermute | solution.py:28
  25.9 6.3 collective-permute-start
  32.4 7.4 %collective-permute-start.3 = (bf16[16,1,10,384]{3,2,1,0:T(8,128)(2,1)S(1)}, bf16[16,1,10,384]{3,2,1,0:T(8,128)(2,1)S(1)}, u32[]{:S(2)}, u32[]{:S(2)}) collective-permute-start(bf16[16,1,10,384]{3,2,1,0:T(8,128)(2,1)S(1)} %get-tuple-element.86), channel_id=1, source_target_pairs={{1,0},{3,2},{5,4},{7,6},{9,8},{11,10},{13,12},{15,14},{17,16},{19,... | collective-permute-start | bytes 368648 | tf_op jit(solution)/shard_map/ppermute | solution.py:28
  33.7 7.6 %collective-permute-start.2 = (bf16[16,1,10,384]{3,2,1,0:T(8,128)(2,1)S(1)}, bf16[16,1,10,384]{3,2,1,0:T(8,128)(2,1)S(1)}, u32[]{:S(2)}, u32[]{:S(2)}) collective-permute-start(bf16[16,1,10,384]{3,2,1,0:T(8,128)(2,1)S(1)} %get-tuple-element.87), channel_id=1, source_target_pairs={{0,1},{2,3},{4,5},{6,7},{8,9},{10,11},{12,13},{14,15},{16,17},{18,... | collective-permute-start | bytes 368648 | tf_op jit(solution)/shard_map/ppermute | solution.py:26
  58.1 9.2 %collective-permute-start.5 = (bf16[16,8,1,384]{3,2,1,0:T(2,128)(2,1)S(1)}, bf16[16,8,1,384]{3,2,1,0:T(2,128)(2,1)S(1)}, u32[]{:S(2)}, u32[]{:S(2)}) collective-permute-start(bf16[16,8,1,384]{3,2,1,0:T(2,128)(2,1)S(1)} %get-tuple-element.93), channel_id=1, source_target_pairs={{2,0},{4,2},{6,4},{8,6},{10,8},{12,10},{14,12},{3,1},{5,3},{7,5},{... | collective-permute-start | bytes 294920 | tf_op jit(solution)/shard_map/ppermute | solution.py:28
  60.0 8.1 %collective-permute-start.4 = (bf16[16,8,1,384]{3,2,1,0:T(2,128)(2,1)S(1)}, bf16[16,8,1,384]{3,2,1,0:T(2,128)(2,1)S(1)}, u32[]{:S(2)}, u32[]{:S(2)}) collective-permute-start(bf16[16,8,1,384]{3,2,1,0:T(2,128)(2,1)S(1)} %get-tuple-element.92), channel_id=1, source_target_pairs={{0,2},{2,4},{4,6},{6,8},{8,10},{10,12},{12,14},{1,3},{3,5},{5,7},{... | collective-permute-start | bytes 294920 | tf_op jit(solution)/shard_map/ppermute | solution.py:26
  68.3 7.3 %collective-permute-start.7 = (bf16[16,1,10,384]{3,2,1,0:T(8,128)(2,1)S(1)}, bf16[16,1,10,384]{3,2,1,0:T(8,128)(2,1)S(1)}, u32[]{:S(2)}, u32[]{:S(2)}) collective-permute-start(bf16[16,1,10,384]{3,2,1,0:T(8,128)(2,1)S(1)} %get-tuple-element.83), channel_id=1, source_target_pairs={{1,0},{3,2},{5,4},{7,6},{9,8},{11,10},{13,12},{15,14},{17,16},{19,... | collective-permute-start | bytes 368648 | tf_op jit(solution)/shard_map/ppermute | solution.py:28
  69.6 6.9 %collective-permute-start.6 = (bf16[16,1,10,384]{3,2,1,0:T(8,128)(2,1)S(1)}, bf16[16,1,10,384]{3,2,1,0:T(8,128)(2,1)S(1)}, u32[]{:S(2)}, u32[]{:S(2)}) collective-permute-start(bf16[16,1,10,384]{3,2,1,0:T(8,128)(2,1)S(1)} %get-tuple-element.82), channel_id=1, source_target_pairs={{0,1},{2,3},{4,5},{6,7},{8,9},{10,11},{12,13},{14,15},{16,17},{18,... | collective-permute-start | bytes 368648 | tf_op jit(solution)/shard_map/ppermute | solution.py:26
  83.9 2.7 copy-start.9
  119.0 1.5 copy-start.32
  355.0 2.3 copy-start.36
  357.3 1.8 copy-start.39
  359.1 1.8 copy-start.38
  360.9 1.8 copy-start.35
  362.7 1.9 copy-start.34
  364.6 1.8 copy-start.33
  366.4 1.8 copy-start.27
  368.2 1.9 copy-start.26
  370.1 1.9 copy-start.25
  370.1 3.7 copy-start.24
  370.1 5.5 copy-start.23
  371.9 14.5 %slice-start = ((s8[9437184]{0:T(1024)(128)(4,1)}), s8[4194304]{0:T(1024)(128)(4,1)S(1)}, s32[]{:S(2)}) async-start(s8[9437184]{0:T(1024)(128)(4,1)} %bitcast.383), calls=%async_computation.4 | async-start | bytes 8388608
  373.7 3.6 copy-start.22
  375.6 10.8 %slice-start.1 = ((s8[9437184]{0:T(1024)(128)(4,1)}), s8[4194304]{0:T(1024)(128)(4,1)S(1)}, s32[]{:S(2)}) async-start(s8[9437184]{0:T(1024)(128)(4,1)} %bitcast.383), calls=%async_computation.5 | async-start | bytes 8388608
  377.4 1.8 copy-start.21
  379.2 1.8 copy-start.20
  381.0 1.8 copy-start.19
  381.0 5.4 slice-start.2
  382.8 1.8 copy-start.18
  386.4 4.5 copy-start.17
  391.0 1.8 copy-start.16
  392.8 1.8 copy-start.15
  394.6 1.8 copy-start.14
  396.4 1.9 copy-start.13
  398.3 1.8 copy-start.12
  400.1 1.9 copy-start.11
  402.0 1.8 copy-start.10
  403.8 1.8 copy-start.5
  422.0 2.7 copy-start.31
  430.5 16.5 %copy-start.40 = (f32[384,32]{1,0:T(8,128)S(1)}, f32[384,32]{1,0:T(8,128)}, u32[]{:S(2)}) copy-start(f32[384,32]{1,0:T(8,128)} %fusion.104) | copy-start | bytes 147460
  461.2 218.9 %copy-start.1 = (bf16[384,32]{0,1:T(8,128)(2,1)S(1)}, bf16[384,32]{0,1:T(8,128)(2,1)}, u32[]{:S(2)}) copy-start(bf16[384,32]{0,1:T(8,128)(2,1)} %param.13) | copy-start | bytes 73732
  461.2 20.6 %all-to-all-start.1 = ((bf16[1,16,8,8,384]{4,3,2,0,1:T(8,128)(2,1)}), bf16[1,16,8,8,384]{4,3,2,0,1:T(8,128)(2,1)S(1)}, u32[]{:S(2)}, u32[]{:S(2)}) async-start(bf16[1,16,8,8,384]{4,3,2,0,1:T(8,128)(2,1)} %bitcast.63), calls=%async_computation.1 | async-start | bytes 1572864 | tf_op jit(solution)/shard_map/all_to_all | solution.py:157
  (13 other events, 16.4 us)
Sparse Core Ops, SparseCore 0:
  9.7 320.8 all-gather.1
  458.3 218.5 all-reduce.4
where the time goes:
time: 692 us; the launch traced here: 687 us
  waiting for transfers between devices  425 us (61%)
  matrix products  107 us (15%)
  local copies, waits for them, and re-layouts  72.1 us (10%)
  starting transfers between devices  34.9 us (5%)
  other arithmetic  32.3 us (5%)
  between operations  16 us (2%)
    all_gather x1, waiting for transfers between devices, per_device(): lax.all_gather(conv_weight, ('dp', 'tm', 'height'), axis=0, tiled=True)  209 us
    unnamed x3, waiting for transfers between devices  195 us
    dot_general x27, matrix products, per_device(): lax.dot_general(back_window, weight_piece[:, number, :], (((1,), (1,)), (...  62.4 us
    dot_general x27, matrix products, per_device(): lax.dot_general(window, grad_conv, (((0,), (0,)), ((), ())), preferred_el...  41.6 us
    slice x2, local copies, waits for them, and re-layouts, per_device(): weight_piece[:, number, :]  28.3 us
    ppermute x4, starting transfers between devices, padded(): lax.ppermute(tail, axis, [(i, (i + 1) % count) for i in range(ends)])  17 us
    reshape x1, local copies, waits for them, and re-layouts, per_device(): conv_part = jnp.stack(pieces, axis=1).reshape(row_count, 27 * channels)  16.5 us
    all_to_all x1, waiting for transfers between devices, per_device(): lax.all_to_all(input_grad, 'tm', split_axis=1, concat_axis=3, tiled=True)  16.2 us
  transfers between devices with their start and end apart: 12, of which 9 were waited for; matrix products, arithmetic and copies ran while one was open for 11% of the time, Pallas kernels for 0%

commit v1 on v0

v1 whole, which is shorter than its diff:
```python
import math

import jax
import jax.numpy as jnp
import numpy as np
from jax import lax
from jax.experimental import pallas as pl
from jax.experimental.pallas import tpu as pltpu
from jax.sharding import PartitionSpec as P

MESH = pl.DeviceIdType.MESH
F32 = jnp.float32
BF16 = jnp.bfloat16
EPSILON = 1e-06
ROOT_THREE = math.sqrt(3.0)
SCALING = 1.0 / math.sqrt(131072.0)
C = 384
AXES = ((0, 1, 2), (1, 2, 0), (2, 0, 1))
NT = (((1,), (1,)), ((), ()))
TN = (((0,), (0,)), ((), ()))


def channel_of(x, y, z, core, r):
    return (x // 2) * 192 + y * 48 + z * 12 + core * 6 + (x % 2) * 3 + r


def order_tables():
    tables = np.zeros((3, C, C), np.float32)
    for group, axes in enumerate(AXES):
        for row in range(C):
            place = {axes[0]: row // 96, axes[1]: row // 24 % 4, axes[2]: row // 6 % 4}
            chan = channel_of(place[0], place[1], place[2], row // 3 % 2, row % 3)
            tables[group, row, chan] = 1.0
    return tables


def swap_table():
    table = np.zeros((256, 256), np.float32)
    for tap in range(16):
        for chan in range(16):
            table[tap * 16 + chan, chan * 16 + tap] = 1.0
    return table


def fold_table():
    table = np.zeros((256, 32), np.float32)
    for lane in range(128):
        table[lane, lane % 16] = 1.0
        table[128 + lane, 16 + lane % 16] = 1.0
    return table


def mod(value, base):
    guess = (value.astype(F32) * (1.0 / base)).astype(jnp.int32)
    left = value - guess * base
    left = jnp.where(left < 0, left + base, left)
    return jnp.where(left >= base, left - base, left)


def sigmoid(value):
    return 1.0 / (1.0 + jnp.exp(-value))


def kernel(
    seeds, lengths, bout, lgrad, hw, hwt, binp, wsh, order, swap, fold,
    out_ig, out_cg, out_hg,
    wg, wt, gs, hs, rg, rh, grid, act3, act_t, hpart, hpart_in,
    sb, r1, sum1, r2, p3, r3, fin, fin_in, ybuf,
    ag_s, ag_r, g_s, g_r, gf_s, gf_r, h_s, h_r, hf_s, hf_r, own_sem,
    d2d_s, d2d_r, c1_s, c1_r, c2_s, c2_r, c3_s, c3_r,
):
    dp = lax.axis_index("dp")
    tm = lax.axis_index("tm")
    xl = lax.axis_index("height")
    xh = lax.div(dp, 4)
    y = lax.rem(dp, 4)
    z = lax.div(tm, 2)
    core = lax.rem(tm, 2)
    x = xh * 2 + xl

    def dev(x_, y_, z_, core_):
        return (lax.div(x_, 2) * 4 + y_, z_ * 2 + core_, lax.rem(x_, 2))

    def peer(axis, step):
        place = [x, y, z]
        place[axis] = lax.rem(place[axis] + step, 4)
        return dev(*place, core)

    partner = dev(x, y, z, 1 - core)

    def halo_peer(step):
        return dev(xh * 2 + 1 - xl, y, lax.rem(z + step, 4), core)

    def send(src, dst, s_sem, r_sem, where):
        copy = pltpu.make_async_remote_copy(
            src_ref=src, dst_ref=dst, send_sem=s_sem, recv_sem=r_sem,
            device_id=where, device_id_type=MESH,
        )
        copy.start()
        return copy

    sent = []

    barrier = pltpu.get_barrier_semaphore()
    friends = [peer(axis, step) for axis in range(3) for step in (1, 2, 3)]
    friends.append(partner)
    friends += [halo_peer(step) for step in (1, 2, 3)]
    for friend in friends:
        pl.semaphore_signal(barrier, inc=1, device_id=friend, device_id_type=MESH)
    pl.semaphore_wait(barrier, len(friends))

    ag1 = []
    for half in range(2):
        wg[half, xh, y, z, core, xl] = wsh[half]
        for step in (2, 1, 3):
            n = half * 3 + step - 1
            ag1.append(
                send(wsh.at[half], wg.at[half, xh, y, z, core, xl], ag_s.at[n], ag_r.at[n], peer(2, step))
            )

    gs[16:18] = jnp.zeros((2, 64, C), BF16)
    hs[128:144] = jnp.zeros((16, C), BF16)
    hpart[...] = jnp.zeros((C, 128), F32)
    seed = seeds[0]
    length = lengths[0]

    def head_block(blk, carry):
        rows = pl.multiple_of(blk * 128, 128)
        values = bout[pl.ds(rows, 128), :].astype(F32)
        inverse = lax.rsqrt(jnp.mean(values * values, axis=-1, keepdims=True) + EPSILON)
        normed = values * inverse
        logistic = sigmoid(normed)
        active_out = (normed * logistic).astype(BF16)
        latent = jnp.dot(active_out, hw[...], preferred_element_type=F32)
        lines = pl.multiple_of(blk * 16, 16)
        upstream = lgrad[pl.ds(lines, 16), :]
        line = lax.broadcasted_iota(jnp.int32, (16, 128), 0) + blk * 16
        lane = lax.broadcasted_iota(jnp.int32, (16, 128), 1)
        position = (line + (line >> 3) * 8 + xl * 8) * 1024 + tm * 128 + lane
        primary = mod(seed * 7919 + position, 30269)
        primary = mod(primary * primary + 7, 30269)
        primary = mod(primary * primary + 101, 30269)
        secondary = mod(seed * 7907 + position * 3, 30307)
        secondary = mod(secondary * secondary + 13, 30307)
        secondary = mod(secondary * secondary + 211, 30307)
        combined = mod(primary + secondary, 30269)
        noise = ROOT_THREE * ((combined.astype(F32) + 0.5) * (2.0 / 30269.0) - 1.0)
        pick = lax.broadcasted_iota(jnp.int32, (1, 8, 128), 2) >> 4 == lax.broadcasted_iota(
            jnp.int32, (1, 8, 128), 1
        )

        def spread(part):
            wide = jnp.broadcast_to(part.reshape(16, 1, 128), (16, 8, 128))
            return jnp.where(pick, wide, 0.0).reshape(128, 128)

        both = jnp.concatenate([spread(upstream), spread(0.5 * upstream * noise)], axis=1)
        sides = jnp.dot(both, fold[...], precision=lax.Precision.HIGHEST, preferred_element_type=F32)
        frame = (lax.broadcasted_iota(jnp.int32, (128, 32), 0) >> 6) + blk * 2
        valid = jnp.where(frame < length, 1.0, 0.0)
        is_mean = lax.broadcasted_iota(jnp.int32, (128, 32), 1) < 16
        head_in = valid * jnp.where(
            is_mean, sides + latent, sides * jnp.exp(0.5 * latent) + 0.5 * (jnp.exp(latent) - 1.0)
        )
        head_in = head_in.astype(BF16)
        hpart[:, 0:32] += lax.dot_general(active_out, head_in, TN, preferred_element_type=F32)
        grad = jnp.dot(head_in, hwt[...], preferred_element_type=F32)
        grad = grad * (logistic * (1.0 + normed * (1.0 - logistic)))
        grad = inverse * (grad - normed * jnp.mean(grad * normed, axis=-1, keepdims=True))
        gs[pl.ds(blk * 2, 2)] = grad.astype(BF16).reshape(2, 64, C)
        cells = grad.reshape(2, 8, 8, C)
        border = jnp.where(xl == 0, cells[:, 7], cells[:, 0]).reshape(16, C)
        hs[pl.ds(lines, 16), :] = border.astype(BF16)
        return carry

    lax.fori_loop(0, 8, head_block, 0)

    def frames_of(where):
        return gs.at[pl.ds(where * 4, 6)]

    def border_of(where):
        return hs.at[pl.ds(pl.multiple_of(where * 32, 16), 48), :]

    g_copies = []
    for step in (2, 1, 3):
        g_copies.append(
            send(frames_of(lax.rem(z + step, 4)), rg.at[tm], g_s.at[step], g_r.at[step], peer(2, step))
        )
    g_forward = [send(frames_of(z), rg.at[tm], gf_s.at[0], gf_r.at[0], partner)]
    own = pltpu.make_async_copy(frames_of(z), rg.at[tm], own_sem)
    own.start()
    h_copies = []
    for step in (2, 1, 3, 0):
        h_copies.append(
            send(border_of(lax.rem(z + step, 4)), rh.at[tm], h_s.at[step], h_r.at[step], halo_peer(step))
        )
    hp_copy = send(hpart, hpart_in, d2d_s.at[0], d2d_r.at[0], partner)

    for copy in ag1:
        copy.wait()
    ag2 = []
    for half, axis in ((0, 0), (1, 1)):
        for step in (2, 1, 3):
            n = 6 + half * 3 + step - 1
            held = wg.at[half, xh, y, :, core, xl]
            ag2.append(send(held, held, ag_s.at[n], ag_r.at[n], peer(axis, step)))

    def active_block(blk, carry):
        rows = pl.multiple_of(blk * 64, 64)
        values = binp[pl.ds(rows, 64), :].astype(F32)
        inverse = lax.rsqrt(jnp.mean(values * values, axis=-1, keepdims=True) + EPSILON)
        normed = values * inverse
        active = normed * sigmoid(normed)
        column = lax.broadcasted_iota(jnp.int32, (64, C), 0)
        act3[0, pl.ds(rows, 64), :] = jnp.where(column == 0, 0.0, pltpu.roll(active, 1, 0)).astype(BF16)
        act3[1, pl.ds(rows, 64), :] = active.astype(BF16)
        act3[2, pl.ds(rows, 64), :] = jnp.where(column == 63, 0.0, pltpu.roll(active, 63, 0)).astype(BF16)
        return carry

    lax.fori_loop(0, 16, active_block, 0)
    half_cells = pl.ds(pl.multiple_of(core * 1024, 1024), 1024)
    for group in range(3):
        turned = lax.dot_general(order[group], act3[group], NT, preferred_element_type=F32)
        act_t[group, :, half_cells] = turned.astype(BF16)
    mine = act_t.at[:, :, half_cells]
    act_copy = send(mine, mine, d2d_s.at[1], d2d_r.at[1], partner)

    for copy in ag2:
        copy.wait()
    ag3 = []
    for half, axis in ((0, 1), (1, 0)):
        held = wg.at[0, :, y, :, core, :] if half == 0 else wg.at[1, xh, :, :, core, xl]
        for step in (2, 1, 3):
            n = 12 + half * 3 + step - 1
            ag3.append(send(held, held, ag_s.at[n], ag_r.at[n], peer(axis, step)))

    h_forward = []
    for copy, step in zip(h_copies, (2, 1, 3, 0)):
        copy.wait_recv()
        slot = rh.at[lax.rem(z + 4 - step, 4) * 2 + core]
        h_forward.append(send(slot, slot, hf_s.at[step], hf_r.at[step], partner))
    for copy, step in reversed(list(zip(g_copies, (2, 1, 3)))):
        copy.wait_recv()
        slot = rg.at[lax.rem(z + 4 - step, 4) * 2 + core]
        g_forward.append(send(slot, slot, gf_s.at[step], gf_r.at[step], partner))
    own.wait()
    for copy in g_forward + h_forward:
        copy.wait_recv()

    def place_frame(f, carry):
        for pair in range(4):
            left = rg[2 * pair, f].astype(F32).reshape(8, 8, C)
            right = rg[2 * pair + 1, f].astype(F32).reshape(8, 8, C)
            grid[f, 1:9, pair * 16 : pair * 16 + 16, :] = jnp.concatenate([left, right], axis=1).astype(BF16)
        return carry

    lax.fori_loop(0, 6, place_frame, 0)
    near = 9 - 9 * xl
    for pair in range(4):
        left = rh[2 * pair].astype(F32).reshape(6, 8, C)
        right = rh[2 * pair + 1].astype(F32).reshape(6, 8, C)
        grid[:, near, pair * 16 : pair * 16 + 16, :] = jnp.concatenate([left, right], axis=1).astype(BF16)
    grid[:, 9 - near] = jnp.zeros((6, 64, C), BF16)

    coords = (x, y, z)
    act_copy.wait_recv()

    def window(spot):
        i = lax.div(spot, 3)
        j = lax.rem(spot, 3)
        return grid[pl.ds(2 - i, 4), pl.ds(2 - j, 8)].reshape(2048, C)

    c1 = []

    def scatter(s, group, count):
        axis = AXES[group][0]
        for step in (2, 1, 3):
            target = lax.rem(coords[axis] + step, 4)
            c1.append(
                send(
                    sb.at[s, target, 0:count], r1.at[s, step - 1, 0:count],
                    c1_s.at[s, step - 1], c1_r.at[s, step - 1], peer(axis, step),
                )
            )

    def tap_pairs(u):
        for group in range(3):
            s = 3 * u + group
            first = core * 5 + 2 * u
            both = jnp.concatenate([window(first), window(first + 1)], axis=1)
            res = jnp.dot(act_t[group], both, preferred_element_type=F32).astype(BF16)
            sb[s, :, 0] = res[:, :C].reshape(4, 96, C)
            sb[s, :, 1] = res[:, C:].reshape(4, 96, C)
            scatter(s, group, 2)

    tap_pairs(0)
    for copy in ag3:
        copy.wait()
    held = wg.at[:, :, :, :, core]
    w_copy = send(held, held, d2d_s.at[2], d2d_r.at[2], partner)
    tap_pairs(1)

    def single(group):
        res = jnp.dot(act_t[group], window(4), preferred_element_type=F32)
        sb[6 + group, :, 0] = res.astype(BF16).reshape(4, 96, C)

    hp_copy.wait_recv()

    @pl.when(core == 0)
    def _():
        single(0)
        single(1)
        sb[8, :, 0] = jnp.zeros((4, 96, C), BF16)

    @pl.when(core == 1)
    def _():
        whole = hpart[...] + hpart_in[...]
        ordered = jnp.dot(
            order[0].astype(F32), whole, precision=lax.Precision.HIGHEST, preferred_element_type=F32
        )
        sb[6, :, 0] = jnp.concatenate([ordered, jnp.zeros((C, 256), F32)], axis=1).astype(BF16).reshape(4, 96, C)
        sb[7, :, 0] = jnp.zeros((4, 96, C), BF16)
        single(2)

    for group in range(3):
        scatter(6 + group, group, 1)

    w_copy.wait_recv()

    def turn_weights(blk, carry):
        a = lax.div(blk, 12)
        b = lax.rem(lax.div(blk, 3), 4)
        third = lax.rem(blk, 3)
        rows = pl.multiple_of(blk * 16, 16)
        for half in range(2):
            unit = wt_src(half, a, b, third)
            turned = jnp.dot(swap[...], unit, preferred_element_type=F32).astype(BF16)
            for tap in range(16 if half == 0 else 11):
                k = half * 16 + tap
                spot, group = k // 3, k % 3
                wt[group, pl.ds(rows, 16), spot * C : (spot + 1) * C] = turned[tap * 16 : tap * 16 + 16]
        return carry

    flat = wg.reshape(2, C, 16, C)

    def wt_src(half, a, b, third):
        start = a * 192 + b * 48 + third * 16
        return flat[half, pl.ds(start, 16)].reshape(256, C)

    lax.fori_loop(0, 24, turn_weights, 0)

    weights = wt[...].reshape(3 * C, 9 * C)

    def grad_act(f):
        base = core * 2 + f + 2
        cells = [grid[base - k // 3, 2 - k % 3 : 10 - k % 3].reshape(512, C) for k in range(9)]
        ybuf[f] = lax.dot_general(
            jnp.concatenate(cells, axis=1), weights, NT, preferred_element_type=F32
        )

    grad_act(0)

    for copy in c1:
        copy.wait_recv()
    c2 = []
    for group in range(3):
        lead = coords[AXES[group][0]]
        for u in range(3):
            s = 3 * u + group
            for e in range(2 if u < 2 else 1):
                total = sb[s, lead, e].astype(F32)
                for step in range(3):
                    total = total + r1[s, step, e].astype(F32)
                sum1[group, 2 * u + e] = total
        axis = AXES[group][1]
        for step in (2, 1, 3):
            target = lax.rem(coords[axis] + step, 4)
            c2.append(
                send(
                    sum1.at[group, :, pl.ds(pl.multiple_of(target * 24, 8), 24), :], r2.at[group, step - 1],
                    c2_s.at[group, step - 1], c2_r.at[group, step - 1], peer(axis, step),
                )
            )

    grad_act(1)

    for copy in c2:
        copy.wait_recv()
    c3 = []
    for group in range(3):
        spot = coords[AXES[group][1]]
        for n in range(5):
            total = sum1[group, n, pl.ds(pl.multiple_of(spot * 24, 8), 24), :]
            for step in range(3):
                total = total + r2[group, step, n]
            for a in range(4):
                p3[group, a, n] = jnp.concatenate([total[a * 6 : a * 6 + 6], jnp.zeros((2, C), F32)], axis=0)
        axis = AXES[group][2]
        for step in (2, 1, 3):
            target = lax.rem(coords[axis] + step, 4)
            c3.append(
                send(
                    p3.at[group, target], r3.at[group, step - 1],
                    c3_s.at[group, step - 1], c3_r.at[group, step - 1], peer(axis, step),
                )
            )

    def input_block(blk, carry):
        f = lax.div(blk, 8)
        row = lax.rem(blk, 8)
        rows = pl.multiple_of(blk * 64, 64)
        lines = pl.multiple_of(row * 64, 64)
        values = binp[pl.ds(rows, 64), :].astype(F32)
        inverse = lax.rsqrt(jnp.mean(values * values, axis=-1, keepdims=True) + EPSILON)
        normed = values * inverse
        logistic = sigmoid(normed)
        column = lax.broadcasted_iota(jnp.int32, (64, C), 0)
        after = pltpu.roll(ybuf[f, pl.ds(lines, 64), 0:C], 63, 0)
        before = pltpu.roll(ybuf[f, pl.ds(lines, 64), 2 * C : 3 * C], 1, 0)
        grad = (
            jnp.where(column == 63, 0.0, after)
            + ybuf[f, pl.ds(lines, 64), C : 2 * C]
            + jnp.where(column == 0, 0.0, before)
        )
        grad = grad * (logistic * (1.0 + normed * (1.0 - logistic)))
        grad = inverse * (grad - normed * jnp.mean(grad * normed, axis=-1, keepdims=True))
        direct = grid[core * 2 + f, row + 1].astype(F32)
        out_ig[pl.ds(rows, 64), :] = (direct + grad).astype(BF16)
        return carry

    lax.fori_loop(0, 16, input_block, 0)

    for copy in c3:
        copy.wait_recv()
    for group in range(3):
        spot = coords[AXES[group][2]]
        for n in range(5):
            fin[group, n] = (p3[group, spot, n] + r3[group, 0, n]) + (r3[group, 1, n] + r3[group, 2, n])
    last = send(fin, fin_in, d2d_s.at[3], d2d_r.at[3], partner)
    last.wait_recv()

    def result(holder, group, n):
        value = jnp.where(core == holder, fin[group, n], fin_in[group, n])
        return jnp.where(core == 0, value[0:3], value[3:6]) * SCALING

    for k in range(27):
        if k < 14:
            holder, n = 0, k // 3
        elif k == 14:
            holder, n = 1, 4
        else:
            holder, n = 1, (k - 15) // 3
        out_cg[:, k, :] = result(holder, k % 3, n)
    out_hg[...] = result(1, 0, 4)[:, 0:32]

    for copy in g_copies + g_forward + h_copies + h_forward + c1 + c2 + c3:
        copy.wait_send()
    for copy in (hp_copy, act_copy, w_copy, last):
        copy.wait_send()


def per_device(block_input, block_output, latent_grad, seeds, lengths, conv_weight, head_weight):
    wsh = jnp.pad(conv_weight, ((0, 0), (0, 5), (0, 0))).reshape(3, 2, 16, C).transpose(1, 0, 2, 3)
    order = jnp.asarray(order_tables(), BF16)
    swap = jnp.asarray(swap_table(), BF16)
    fold = jnp.asarray(fold_table(), F32)
    vmem = pl.BlockSpec(memory_space=pltpu.VMEM)
    smem = pl.BlockSpec(memory_space=pltpu.SMEM)
    dma = pltpu.SemaphoreType.DMA
    input_grad, conv_grad, head_grad = pl.pallas_call(
        kernel,
        out_shape=(
            jax.ShapeDtypeStruct((1024, C), BF16),
            jax.ShapeDtypeStruct((3, 27, C), F32),
            jax.ShapeDtypeStruct((3, 32), F32),
        ),
        in_specs=[smem, smem] + [vmem] * 9,
        out_specs=(vmem, vmem, vmem),
        scratch_shapes=[
            pltpu.VMEM((2, 2, 4, 4, 2, 2, 3, 16, C), BF16),
            pltpu.VMEM((3, C, 9 * C), BF16),
            pltpu.VMEM((18, 64, C), BF16),
            pltpu.VMEM((144, C), BF16),
            pltpu.VMEM((8, 6, 64, C), BF16),
            pltpu.VMEM((8, 48, C), BF16),
            pltpu.VMEM((6, 10, 64, C), BF16),
            pltpu.VMEM((3, 1024, C), BF16),
            pltpu.VMEM((3, C, 2048), BF16),
            pltpu.VMEM((C, 128), F32),
            pltpu.VMEM((C, 128), F32),
            pltpu.VMEM((9, 4, 2, 96, C), BF16),
            pltpu.VMEM((9, 3, 2, 96, C), BF16),
            pltpu.VMEM((3, 5, 96, C), F32),
            pltpu.VMEM((3, 3, 5, 24, C), F32),
            pltpu.VMEM((3, 4, 5, 8, C), F32),
            pltpu.VMEM((3, 3, 5, 8, C), F32),
            pltpu.VMEM((3, 5, 8, C), F32),
            pltpu.VMEM((3, 5, 8, C), F32),
            pltpu.VMEM((2, 512, 3 * C), F32),
            dma((18,)), dma((18,)),
            dma((4,)), dma((4,)), dma((4,)), dma((4,)),
            dma((4,)), dma((4,)), dma((4,)), dma((4,)),
            dma,
            dma((4,)), dma((4,)),
            dma((9, 3)), dma((9, 3)),
            dma((3, 3)), dma((3, 3)),
            dma((3, 3)), dma((3, 3)),
        ],
        compiler_params=pltpu.CompilerParams(
            collective_id=0, has_side_effects=True, vmem_limit_bytes=63 * 2**20
        ),
        name="autoencoder_backward",
    )(
        seeds, lengths, block_output.reshape(1024, C), latent_grad.reshape(128, 128),
        head_weight, head_weight.T, block_input.reshape(1024, C), wsh, order, swap, fold,
    )
    return (input_grad.reshape(block_input.shape), conv_grad, head_grad)


def solution(mesh):
    placed = (
        P("dp", "tm", "height", None, None),
        P("dp", None, "height", "tm", None),
        P("dp", None, "height", "tm"),
        P("dp"),
        P("dp"),
        P(("dp", "tm", "height"), None, None),
        P(),
    )
    return jax.shard_map(
        per_device,
        mesh=mesh,
        in_specs=placed,
        out_specs=(
            P("dp", "tm", "height", None, None),
            P(("dp", "tm", "height"), None, None),
            P(("dp", "tm", "height"), None),
        ),
        check_vma=False,
    )
```

time: 692 us -> 104 us (0.15)
  waiting for transfers between devices: 425 us -> 0 us
  matrix products: 107 us -> 0 us
  Pallas kernels: 0 us -> 95.8 us
  local copies, waits for them, and re-layouts: 72.1 us -> 5.77 us
  starting transfers between devices: 34.9 us -> 0 us
  other arithmetic: 32.3 us -> 0 us
  between operations: 16 us -> 1.95 us
    all_gather x1 -> x0, waiting for transfers between devices: 209 us -> none  [per_device(): lax.all_gather(conv_weight, ('dp', 'tm', 'height'), axis=0, tiled=True)]
    unnamed x3 -> x0, waiting for transfers between devices: 195 us -> none
    dot_general x57 -> x0, matrix products: 107 us -> none  [the longest x27 62.4 us: per_device(): lax.dot_general(back_window, weight_piece[:, number, :], (((1,), (1,)), (...]
    pallas_call x0 -> x1, Pallas kernels: none -> 95.8 us  [per_device(): pl.pallas_call(kernel, out_shape=(jax.ShapeDtypeStruct((1024, C), BF16),...]
    slice x8 -> x0, local copies, waits for them, and re-layouts: 39.8 us -> none  [the longest x2 28.3 us: per_device(): weight_piece[:, number, :]]
    ppermute x8 -> x0, starting transfers between devices: 23.5 us -> none  [the longest x4 17 us: padded(): lax.ppermute(tail, axis, [(i, (i + 1) % count) for i in range(ends)])]
    reshape x2 -> x1, local copies, waits for them, and re-layouts: 17.2 us -> 0.64 us  [per_device(): jnp.pad(conv_weight, ((0, 0), (0, 5), (0, 0))).reshape(3, 2, 16, C)]
    all_to_all x2 -> x0, waiting for transfers between devices: 16.2 us -> none  [the longest x1 16.2 us: per_device(): lax.all_to_all(input_grad, 'tm', split_axis=1, concat_axis=3, tiled=True)]
  transfers between devices with their start and end apart: 12 -> 0, of which waited for: 9 -> 0; matrix products, arithmetic and copies ran while one was open for 11% -> 0% of each run, Pallas kernels for 0% -> 0%
where the time goes in v1:
time: 104 us
  Pallas kernels  95.8 us (92%)
  local copies, waits for them, and re-layouts  5.77 us (6%)
  between operations  1.95 us (2%)
    pallas_call x1, Pallas kernels, per_device(): pl.pallas_call(kernel, out_shape=(jax.ShapeDtypeStruct((1024, C), BF16),...  95.8 us
    unnamed x10, local copies, waits for them, and re-layouts  4.23 us

profile of v1, /device:TPU:1, one launch (start us, length us, event | category | flops | bytes accessed | tf_op | source)
XLA Modules:
  0.0 103.5 jit_solution(444504248003032800)
XLA Ops:
  1.9 0.9 pad.4
  2.8 0.0 copy-start.1
  2.8 0.6 copy.17
  3.5 0.1 copy-done.1
  3.6 0.7 copy.15.hw
  4.3 95.8 %autoencoder_backward.1 = (bf16[1024,384]{1,0:T(8,128)(2,1)}, f32[3,27,384]{2,1,0:T(8,128)}, f32[3,32]{1,0:T(4,128)}) custom-call(s32[1]{0:T(128)S(6)} %copy.21.seeds, s32[1]{0:T(128)S(6)} %copy.22.lengths, bf16[1024,384]{1,0:T(8,128)(2,1)} %bitcast.10, f32[128,128]{1,0:T(8,128)} %bitcast.15, bf16[384,32]{1,0:T(8,128)(2,1)} %copy.15.hw, ...), custom_call_target="tpu_custom_call" | custom-call | tf_op jit(solution)/shard_map/autoencoder_backward/pallas_call | solution.py:469
  100.1 0.0 copy-start
  100.1 2.1 %copy.23 = bf16[1,2,8,64,384]{4,3,2,1,0:T(8,128)(2,1)} copy(bf16[1,2,8,64,384]{4,3,2,1,0:T(8,128)(2,1)} %bitcast.9) | data formatting | bytes 1572864
  102.3 0.0 copy-done
  102.3 0.0 copy-start.2
  102.3 0.7 copy.24
  102.9 0.0 copy-done.2
  102.9 0.6 copy.25
Async XLA Ops:
  2.8 0.7 copy-start.1
  100.1 2.1 %copy-start = (f32[3,27,384]{2,1,0:T(8,128)S(1)}, f32[3,27,384]{2,1,0:T(8,128)}, u32[]{:S(2)}) copy-start(f32[3,27,384]{2,1,0:T(8,128)} %get-tuple-element.13) | copy-start | bytes 373252
  102.3 0.7 copy-start.2

commit v2 on v1

v2 whole, which is shorter than its diff:
```python
import math

import jax
import jax.numpy as jnp
import numpy as np
from jax import lax
from jax.experimental import pallas as pl
from jax.experimental.pallas import tpu as pltpu
from jax.sharding import PartitionSpec as P

MESH = pl.DeviceIdType.MESH
F32 = jnp.float32
BF16 = jnp.bfloat16
EPSILON = 1e-06
ROOT_THREE = math.sqrt(3.0)
SCALING = 1.0 / math.sqrt(131072.0)
C = 384
AXES = ((0, 1, 2), (1, 2, 0), (2, 0, 1))
NT = (((1,), (1,)), ((), ()))
TN = (((0,), (0,)), ((), ()))


def channel_of(x, y, z, core, r):
    return (x // 2) * 192 + y * 48 + z * 12 + core * 6 + (x % 2) * 3 + r


def order_tables():
    tables = np.zeros((3, C, C), np.float32)
    for group, axes in enumerate(AXES):
        for row in range(C):
            place = {axes[0]: row // 96, axes[1]: row // 24 % 4, axes[2]: row // 6 % 4}
            chan = channel_of(place[0], place[1], place[2], row // 3 % 2, row % 3)
            tables[group, row, chan] = 1.0
    return tables


def swap_table():
    table = np.zeros((256, 256), np.float32)
    for tap in range(16):
        for chan in range(16):
            table[tap * 16 + chan, chan * 16 + tap] = 1.0
    return table


def pick_table():
    table = np.zeros((2, 16, 27), np.float32)
    for core in range(2):
        for group in range(3):
            for m in range(5):
                tap = 3 * (4 * core + m) + group
                if (tap >= 14) == (core == 1):
                    table[core, group * 5 + m, tap] = 1.0
    return table


def fold_table():
    table = np.zeros((256, 32), np.float32)
    for lane in range(128):
        table[lane, lane % 16] = 1.0
        table[128 + lane, 16 + lane % 16] = 1.0
    return table


def mod(value, base):
    guess = (value.astype(F32) * (1.0 / base)).astype(jnp.int32)
    left = value - guess * base
    left = jnp.where(left < 0, left + base, left)
    return jnp.where(left >= base, left - base, left)


def sigmoid(value):
    return 1.0 / (1.0 + jnp.exp(-value))


def kernel(
    seeds, lengths, bout, lgrad, hwt, binp, cw, order, swap, fold, pick,
    out_ig, out_cg, out_hg,
    ush, wg, wt, gs, hs, rg, rh, grid, act3, act_t, ao, hin, hpart, hpart_in,
    sb, r1, p2, r2, p3, r3, fin, fin_in, ybuf, part, part_in,
    a1_s, a1_r, a2_s, a2_r, a3_s, a3_r, a4_s, a4_r, g_s, g_r, gf_s, gf_r, h_s, h_r, hf_s, hf_r, own_sem,
    d2d_s, d2d_r, c1_s, c1_r, c2_s, c2_r, c3_s, c3_r,
):
    dp = lax.axis_index("dp")
    tm = lax.axis_index("tm")
    xl = lax.axis_index("height")
    xh = lax.div(dp, 4)
    y = lax.rem(dp, 4)
    z = lax.div(tm, 2)
    core = lax.rem(tm, 2)
    x = xh * 2 + xl

    def dev(x_, y_, z_, core_):
        return (lax.div(x_, 2) * 4 + y_, z_ * 2 + core_, lax.rem(x_, 2))

    def peer(axis, step):
        place = [x, y, z]
        place[axis] = lax.rem(place[axis] + step, 4)
        return dev(*place, core)

    partner = dev(x, y, z, 1 - core)

    def halo_peer(step):
        return dev(xh * 2 + 1 - xl, y, lax.rem(z + step, 4), core)

    def across(step):
        return dev(x, y, lax.rem(z + step, 4), 1 - core)

    def send(src, dst, s_sem, r_sem, where):
        copy = pltpu.make_async_remote_copy(
            src_ref=src, dst_ref=dst, send_sem=s_sem, recv_sem=r_sem,
            device_id=where, device_id_type=MESH,
        )
        copy.start()
        return copy

    barrier = pltpu.get_barrier_semaphore()
    friends = [peer(axis, step) for axis in range(3) for step in (1, 2, 3)]
    friends += [across(step) for step in range(4)]
    friends += [halo_peer(step) for step in (1, 2, 3)]
    for friend in friends:
        pl.semaphore_signal(barrier, inc=1, device_id=friend, device_id_type=MESH)

    for taps in range(2):
        for r in range(3):
            ush[taps, r] = jnp.dot(pick[taps], cw[r], preferred_element_type=F32).astype(BF16)

    gs[16:18] = jnp.zeros((2, 64, C), BF16)
    hs[128:144] = jnp.zeros((16, C), BF16)
    seed = seeds[0]
    length = lengths[0]

    def head_block(turn, carry):
        blk = lax.rem(turn + 2 * z + 2, 8)
        rows = pl.multiple_of(blk * 128, 128)
        values = bout[pl.ds(rows, 128), :].astype(F32)
        inverse = lax.rsqrt(jnp.mean(values * values, axis=-1, keepdims=True) + EPSILON)
        normed = values * inverse
        logistic = sigmoid(normed)
        active_out = (normed * logistic).astype(BF16)
        latent = lax.dot_general(active_out, hwt[...], NT, preferred_element_type=F32)
        lines = pl.multiple_of(blk * 16, 16)
        upstream = lgrad[pl.ds(lines, 16), :]
        line = lax.broadcasted_iota(jnp.int32, (16, 128), 0) + blk * 16
        lane = lax.broadcasted_iota(jnp.int32, (16, 128), 1)
        position = (line + (line >> 3) * 8 + xl * 8) * 1024 + tm * 128 + lane
        primary = mod(seed * 7919 + position, 30269)
        primary = mod(primary * primary + 7, 30269)
        primary = mod(primary * primary + 101, 30269)
        secondary = mod(seed * 7907 + position * 3, 30307)
        secondary = mod(secondary * secondary + 13, 30307)
        secondary = mod(secondary * secondary + 211, 30307)
        combined = mod(primary + secondary, 30269)
        noise = ROOT_THREE * ((combined.astype(F32) + 0.5) * (2.0 / 30269.0) - 1.0)
        pick = lax.broadcasted_iota(jnp.int32, (1, 8, 128), 2) >> 4 == lax.broadcasted_iota(
            jnp.int32, (1, 8, 128), 1
        )

        def spread(part):
            wide = jnp.broadcast_to(part.reshape(16, 1, 128), (16, 8, 128))
            return jnp.where(pick, wide, 0.0).reshape(128, 128)

        both = jnp.concatenate([spread(upstream), spread(0.5 * upstream * noise)], axis=1)
        sides = jnp.dot(both, fold[...], precision=lax.Precision.HIGHEST, preferred_element_type=F32)
        frame = (lax.broadcasted_iota(jnp.int32, (128, 32), 0) >> 6) + blk * 2
        valid = jnp.where(frame < length, 1.0, 0.0)
        is_mean = lax.broadcasted_iota(jnp.int32, (128, 32), 1) < 16
        head_in = valid * jnp.where(
            is_mean, sides + latent, sides * jnp.exp(0.5 * latent) + 0.5 * (jnp.exp(latent) - 1.0)
        )
        head_in = head_in.astype(BF16)
        ao[pl.ds(rows, 128), :] = active_out
        hin[pl.ds(rows, 128), :] = head_in
        grad = jnp.dot(head_in, hwt[...], preferred_element_type=F32)
        grad = grad * (logistic * (1.0 + normed * (1.0 - logistic)))
        grad = inverse * (grad - normed * jnp.mean(grad * normed, axis=-1, keepdims=True))
        gs[pl.ds(blk * 2, 2)] = grad.astype(BF16).reshape(2, 64, C)
        cells = grad.reshape(2, 8, 8, C)
        border = jnp.where(xl == 0, cells[:, 7], cells[:, 0]).reshape(16, C)
        hs[pl.ds(lines, 16), :] = border.astype(BF16)
        return carry

    def frames_of(where):
        return gs.at[pl.ds(where * 4, 6)]

    def border_of(where):
        return hs.at[pl.ds(pl.multiple_of(where * 32, 16), 48), :]

    g_copies = []
    h_copies = []

    def send_frames(step):
        target = lax.rem(z + step, 4)
        g_copies.append(send(frames_of(target), rg.at[tm], g_s.at[step], g_r.at[step], peer(2, step)))
        h_copies.append(send(border_of(target), rh.at[tm], h_s.at[step], h_r.at[step], halo_peer(step)))

    lax.fori_loop(0, 1, head_block, 0)
    pl.semaphore_wait(barrier, len(friends))

    ag1 = []
    here = wg.at[xh, y, z, core, xl]
    wg[xh, y, z, core, xl] = ush[core]
    for step in (2, 1, 3):
        ag1.append(send(ush.at[core], here, a1_s.at[step], a1_r.at[step], peer(2, step)))
    for step in (0, 2, 1, 3):
        ag1.append(send(ush.at[1 - core], here, a1_s.at[4 + step], a1_r.at[4 + step], across(step)))

    lax.fori_loop(1, 3, head_block, 0)
    send_frames(1)
    lax.fori_loop(3, 5, head_block, 0)
    send_frames(2)
    lax.fori_loop(5, 7, head_block, 0)
    send_frames(3)
    lax.fori_loop(7, 8, head_block, 0)
    g_forward = [send(frames_of(z), rg.at[tm], gf_s.at[0], gf_r.at[0], partner)]
    own = pltpu.make_async_copy(frames_of(z), rg.at[tm], own_sem)
    own.start()
    h_copies.append(send(border_of(z), rh.at[tm], h_s.at[0], h_r.at[0], halo_peer(0)))

    routes = ((0, 1), (1, 0))

    def chunk(half, near, far):
        place = [x, y]
        place[routes[half][0]] = lax.rem(place[routes[half][0]] + 4 - near, 4)
        place[routes[half][1]] = lax.rem(place[routes[half][1]] + 4 - far, 4)
        return wg.at[lax.div(place[0], 2), place[1], :, half, lax.rem(place[0], 2)]

    ag2 = {}
    ag3 = {}
    ag4 = {}

    def pass_on(half, j):
        block = chunk(half, j, 0)
        for way, step in ((0, 1), (1, 3)):
            ag3[half, j, way] = send(
                block, block, a3_s.at[half, j, way], a3_r.at[half, j, way], peer(routes[half][1], step)
            )

    def relay(j):
        way, step = (0, 1) if j % 2 == 0 else (1, 3)
        for half in range(2):
            ag3[half, j, way].wait_recv()
            block = chunk(half, j, step)
            ag4[half, j] = send(
                block, block, a4_s.at[half, j], a4_r.at[half, j], peer(routes[half][1], step)
            )

    for copy in ag1:
        copy.wait()
    for half in range(2):
        block = chunk(half, 0, 0)
        for step in (2, 1, 3):
            n = step - 1
            ag2[half, step] = send(
                block, block, a2_s.at[half, n], a2_r.at[half, n], peer(routes[half][0], step)
            )
        pass_on(half, 0)

    hpart[...] = jnp.zeros((C, 128), F32)
    hpart[:, 0:32] = lax.dot_general(ao[...], hin[...], TN, preferred_element_type=F32)
    hp_copy = send(hpart, hpart_in, d2d_s.at[0], d2d_r.at[0], partner)

    def active_block(blk, carry):
        rows = pl.multiple_of(blk * 64, 64)
        values = binp[pl.ds(rows, 64), :].astype(F32)
        inverse = lax.rsqrt(jnp.mean(values * values, axis=-1, keepdims=True) + EPSILON)
        normed = values * inverse
        active = normed * sigmoid(normed)
        column = lax.broadcasted_iota(jnp.int32, (64, C), 0)
        act3[0, pl.ds(rows, 64), :] = jnp.where(column == 0, 0.0, pltpu.roll(active, 1, 0)).astype(BF16)
        act3[1, pl.ds(rows, 64), :] = active.astype(BF16)
        act3[2, pl.ds(rows, 64), :] = jnp.where(column == 63, 0.0, pltpu.roll(active, 63, 0)).astype(BF16)
        return carry

    lax.fori_loop(0, 16, active_block, 0)
    half_cells = pl.ds(pl.multiple_of(core * 1024, 1024), 1024)
    for group in range(3):
        turned = lax.dot_general(order[group], act3[group], NT, preferred_element_type=F32)
        act_t[group, :, half_cells] = turned.astype(BF16)
    mine = act_t.at[:, :, half_cells]
    act_copy = send(mine, mine, d2d_s.at[1], d2d_r.at[1], partner)

    for step in (1, 3, 2):
        for half in range(2):
            ag2[half, step].wait_recv()
            pass_on(half, step)

    hp_copy.wait_recv()

    @pl.when(core == 1)
    def _():
        whole = hpart[...] + hpart_in[...]
        ordered = jnp.zeros((C, 128), F32)
        for _ in range(3):
            piece = whole.astype(BF16)
            ordered += jnp.dot(order[0], piece, preferred_element_type=F32)
            whole = whole - piece.astype(F32)
        sb[6, :, 0] = jnp.concatenate([ordered, jnp.zeros((C, 256), F32)], axis=1).astype(BF16).reshape(4, 96, C)

    relay(0)
    h_forward = []
    for g_copy, h_copy, step in zip(g_copies + [None], h_copies, (1, 2, 3, 0)):
        slot = lax.rem(z + 4 - step, 4) * 2 + core
        if g_copy is not None:
            g_copy.wait_recv()
            g_forward.append(send(rg.at[slot], rg.at[slot], gf_s.at[step], gf_r.at[step], partner))
        h_copy.wait_recv()
        h_forward.append(send(rh.at[slot], rh.at[slot], hf_s.at[step], hf_r.at[step], partner))
    relay(1)
    relay(3)
    own.wait()
    for copy in g_forward + h_forward:
        copy.wait_recv()

    def place_frame(f, carry):
        for pair in range(4):
            left = rg[2 * pair, f].astype(F32).reshape(8, 8, C)
            right = rg[2 * pair + 1, f].astype(F32).reshape(8, 8, C)
            grid[f, 1:9, pair * 16 : pair * 16 + 16, :] = jnp.concatenate([left, right], axis=1).astype(BF16)
        return carry

    lax.fori_loop(0, 6, place_frame, 0)
    near = 9 - 9 * xl
    for pair in range(4):
        left = rh[2 * pair].astype(F32).reshape(6, 8, C)
        right = rh[2 * pair + 1].astype(F32).reshape(6, 8, C)
        grid[:, near, pair * 16 : pair * 16 + 16, :] = jnp.concatenate([left, right], axis=1).astype(BF16)
    grid[:, 9 - near] = jnp.zeros((6, 64, C), BF16)

    coords = (x, y, z)
    act_copy.wait_recv()

    def window(spot):
        i = lax.div(spot, 3)
        j = lax.rem(spot, 3)
        return grid[pl.ds(2 - i, 4), pl.ds(2 - j, 8)].reshape(2048, C)

    def scatter(s, group, count):
        axis = AXES[group][0]
        copies = []
        for step in (2, 1, 3):
            target = lax.rem(coords[axis] + step, 4)
            copies.append(
                pltpu.make_async_remote_copy(
                    src_ref=sb.at[s, target, 0:count], dst_ref=r1.at[s, step - 1, 0:count],
                    send_sem=c1_s.at[s, step - 1], recv_sem=c1_r.at[s, step - 1],
                    device_id=peer(axis, step), device_id_type=MESH,
                )
            )
        return copies

    def tap_pairs(u):
        for group in range(3):
            s = 3 * u + group
            first = core * 5 + 2 * u
            both = jnp.concatenate([window(first), window(first + 1)], axis=1)
            res = jnp.dot(act_t[group], both, preferred_element_type=F32).astype(BF16)
            sb[s, :, 0] = res[:, :C].reshape(4, 96, C)
            sb[s, :, 1] = res[:, C:].reshape(4, 96, C)
            for copy in scatter(s, group, 2):
                copy.start()

    users = (None, 0, 1)

    def for_user(group, act):
        if users[group] is None:
            act()
        else:
            pl.when(core == users[group])(act)

    def single(group):
        res = jnp.dot(act_t[group], window(4), preferred_element_type=F32)
        sb[6 + group, :, 0] = res.astype(BF16).reshape(4, 96, C)

    def start_single(group):
        for copy in scatter(6 + group, group, 1):
            copy.start()

    tap_pairs(0)
    relay(2)
    tap_pairs(1)
    pl.when(core == 0)(lambda: single(0))
    start_single(0)
    for group in (1, 2):

        def last_taps(group=group):
            single(group)
            start_single(group)

        for_user(group, last_taps)

    for half in range(2):
        for j in range(4):
            ag3[half, j, 0].wait_recv() if j % 2 else None
            ag3[half, j, 1].wait_recv() if j % 2 == 0 else None
            ag4[half, j].wait_recv()
    flat = wg.reshape(C, 16, C)

    def turn_weights(blk, carry):
        rows = pl.multiple_of(blk * 16, 16)
        unit = flat[pl.ds(rows, 16)].reshape(256, C)
        turned = jnp.dot(swap[...], unit, preferred_element_type=F32).astype(BF16)
        for group in range(3):
            for m in range(5):
                row = (group * 5 + m) * 16
                wt[group, pl.ds(rows, 16), m * C : (m + 1) * C] = turned[row : row + 16]
        return carry

    lax.fori_loop(0, 24, turn_weights, 0, unroll=4)

    weights = wt[...].reshape(3 * C, 5 * C)

    def grad_act(owner):
        cells = []
        for m in range(5):
            spot = 4 * core + m
            i = lax.div(spot, 3)
            j = lax.rem(spot, 3)
            cells.append(grid[pl.ds(owner * 2 + 2 - i, 2), pl.ds(2 - j, 8)].reshape(1024, C))
        ybuf[...] = lax.dot_general(
            jnp.concatenate(cells, axis=1), weights, NT, preferred_element_type=F32
        )

    def shifted(rows):
        column = lax.broadcasted_iota(jnp.int32, (64, C), 0)
        after = pltpu.roll(ybuf[pl.ds(rows, 64), 0:C], 63, 0)
        before = pltpu.roll(ybuf[pl.ds(rows, 64), 2 * C : 3 * C], 1, 0)
        return (
            jnp.where(column == 63, 0.0, after)
            + ybuf[pl.ds(rows, 64), C : 2 * C]
            + jnp.where(column == 0, 0.0, before)
        )

    grad_act(1 - core)

    def part_block(row, carry):
        rows = pl.multiple_of(row * 64, 64)
        part[pl.ds(rows, 64), :] = shifted(rows)
        return carry

    lax.fori_loop(0, 16, part_block, 0)
    part_copy = send(part, part_in, d2d_s.at[2], d2d_r.at[2], partner)

    for s in range(6):
        for copy in scatter(s, s % 3, 2):
            copy.wait_recv()
    for group in range(3):

        def arrived(group=group):
            for copy in scatter(6 + group, group, 1):
                copy.wait_recv()

        for_user(group, arrived)

    c2 = []
    for group in range(3):
        lead = coords[AXES[group][0]]
        if users[group] is not None:

            def blank(group=group):
                sb[6 + group, lead, 0] = jnp.zeros((96, C), BF16)
                for step in range(3):
                    r1[6 + group, step, 0] = jnp.zeros((96, C), BF16)

            pl.when(core != users[group])(blank)
        for a in range(4):
            lines = slice(a * 24, a * 24 + 24)
            totals = []
            for n in range(5):
                s = 3 * (n // 2) + group
                total = sb[s, lead, n % 2, lines].astype(F32)
                for step in range(3):
                    total = total + r1[s, step, n % 2, lines].astype(F32)
                totals.append(total)
            totals.append(jnp.zeros((8, C), F32))
            p2[group, a] = jnp.concatenate(totals, axis=0).astype(BF16)
        axis = AXES[group][1]
        for step in (2, 1, 3):
            target = lax.rem(coords[axis] + step, 4)
            c2.append(
                send(
                    p2.at[group, target], r2.at[group, step - 1],
                    c2_s.at[group, step - 1], c2_r.at[group, step - 1], peer(axis, step),
                )
            )

    grad_act(core)

    for copy in c2:
        copy.wait_recv()
    c3 = []
    for group in range(3):
        spot = coords[AXES[group][1]]
        total = p2[group, spot].astype(F32)
        for step in range(3):
            total = total + r2[group, step].astype(F32)
        for a in range(4):
            rows = [total[n * 24 + a * 6 : n * 24 + a * 6 + 6] for n in range(5)]
            p3[group, a] = jnp.concatenate(rows + [jnp.zeros((2, C), F32)], axis=0).astype(BF16)
        axis = AXES[group][2]
        for step in (2, 1, 3):
            target = lax.rem(coords[axis] + step, 4)
            c3.append(
                send(
                    p3.at[group, target], r3.at[group, step - 1],
                    c3_s.at[group, step - 1], c3_r.at[group, step - 1], peer(axis, step),
                )
            )

    def input_block(blk, carry):
        f = lax.div(blk, 8)
        row = lax.rem(blk, 8)
        rows = pl.multiple_of(blk * 64, 64)
        values = binp[pl.ds(rows, 64), :].astype(F32)
        inverse = lax.rsqrt(jnp.mean(values * values, axis=-1, keepdims=True) + EPSILON)
        normed = values * inverse
        logistic = sigmoid(normed)
        grad = shifted(rows) + part_in[pl.ds(rows, 64), :]
        grad = grad * (logistic * (1.0 + normed * (1.0 - logistic)))
        grad = inverse * (grad - normed * jnp.mean(grad * normed, axis=-1, keepdims=True))
        direct = grid[core * 2 + f, row + 1].astype(F32)
        out_ig[pl.ds(rows, 64), :] = (direct + grad).astype(BF16)
        return carry

    part_copy.wait_recv()
    lax.fori_loop(0, 16, input_block, 0)

    for copy in c3:
        copy.wait_recv()
    for group in range(3):
        spot = coords[AXES[group][2]]
        total = p3[group, spot].astype(F32)
        for step in range(3):
            total = total + r3[group, step].astype(F32)
        fin[group] = total
    last = send(fin, fin_in, d2d_s.at[3], d2d_r.at[3], partner)
    last.wait_recv()

    def result(holder, group, n):
        value = jnp.where(core == holder, fin[group, n * 6 : n * 6 + 6], fin_in[group, n * 6 : n * 6 + 6])
        return jnp.where(core == 0, value[0:3], value[3:6]) * SCALING

    for k in range(27):
        if k < 14:
            holder, n = 0, k // 3
        elif k == 14:
            holder, n = 1, 4
        else:
            holder, n = 1, (k - 15) // 3
        out_cg[:, k, :] = result(holder, k % 3, n)
    out_hg[...] = result(1, 0, 4)[:, 0:32]

    for copy in g_copies + g_forward + h_copies + h_forward + c2 + c3:
        copy.wait_send()
    for s in range(6):
        for copy in scatter(s, s % 3, 2):
            copy.wait_send()
    for group in range(3):

        def left(group=group):
            for copy in scatter(6 + group, group, 1):
                copy.wait_send()

        for_user(group, left)
    for copy in (*ag2.values(), *ag3.values(), *ag4.values(), hp_copy, act_copy, part_copy, last):
        copy.wait_send()


def per_device(block_input, block_output, latent_grad, seeds, lengths, conv_weight, head_weight):
    order = jnp.asarray(order_tables(), BF16)
    swap = jnp.asarray(swap_table(), BF16)
    fold = jnp.asarray(fold_table(), F32)
    pick = jnp.asarray(pick_table(), BF16)
    vmem = pl.BlockSpec(memory_space=pltpu.VMEM)
    smem = pl.BlockSpec(memory_space=pltpu.SMEM)
    dma = pltpu.SemaphoreType.DMA
    input_grad, conv_grad, head_grad = pl.pallas_call(
        kernel,
        out_shape=(
            jax.ShapeDtypeStruct((1024, C), BF16),
            jax.ShapeDtypeStruct((3, 27, C), F32),
            jax.ShapeDtypeStruct((3, 32), F32),
        ),
        in_specs=[smem, smem] + [vmem] * 9,
        out_specs=(vmem, vmem, vmem),
        scratch_shapes=[
            pltpu.VMEM((2, 3, 16, C), BF16),
            pltpu.VMEM((2, 4, 4, 2, 2, 3, 16, C), BF16),
            pltpu.VMEM((3, C, 5 * C), BF16),
            pltpu.VMEM((18, 64, C), BF16),
            pltpu.VMEM((144, C), BF16),
            pltpu.VMEM((8, 6, 64, C), BF16),
            pltpu.VMEM((8, 48, C), BF16),
            pltpu.VMEM((6, 10, 64, C), BF16),
            pltpu.VMEM((3, 1024, C), BF16),
            pltpu.VMEM((3, C, 2048), BF16),
            pltpu.VMEM((1024, C), BF16),
            pltpu.VMEM((1024, 32), BF16),
            pltpu.VMEM((C, 128), F32),
            pltpu.VMEM((C, 128), F32),
            pltpu.VMEM((9, 4, 2, 96, C), BF16),
            pltpu.VMEM((9, 3, 2, 96, C), BF16),
            pltpu.VMEM((3, 4, 128, C), BF16),
            pltpu.VMEM((3, 3, 128, C), BF16),
            pltpu.VMEM((3, 4, 32, C), BF16),
            pltpu.VMEM((3, 3, 32, C), BF16),
            pltpu.VMEM((3, 32, C), F32),
            pltpu.VMEM((3, 32, C), F32),
            pltpu.VMEM((1024, 3 * C), F32),
            pltpu.VMEM((1024, C), F32),
            pltpu.VMEM((1024, C), F32),
            dma((8,)), dma((8,)), dma((2, 3)), dma((2, 3)),
            dma((2, 4, 2)), dma((2, 4, 2)), dma((2, 4)), dma((2, 4)),
            dma((4,)), dma((4,)), dma((4,)), dma((4,)),
            dma((4,)), dma((4,)), dma((4,)), dma((4,)),
            dma,
            dma((4,)), dma((4,)),
            dma((9, 3)), dma((9, 3)),
            dma((3, 3)), dma((3, 3)),
            dma((3, 3)), dma((3, 3)),
        ],
        compiler_params=pltpu.CompilerParams(
            collective_id=0, has_side_effects=True, vmem_limit_bytes=63 * 2**20
        ),
        name="autoencoder_backward",
    )(
        seeds, lengths, block_output.reshape(1024, C), latent_grad.reshape(128, 128),
        head_weight.T, block_input.reshape(1024, C), conv_weight, order, swap, fold, pick,
    )
    return (input_grad.reshape(block_input.shape), conv_grad, head_grad)


def solution(mesh):
    placed = (
        P("dp", "tm", "height", None, None),
        P("dp", None, "height", "tm", None),
        P("dp", None, "height", "tm"),
        P("dp"),
        P("dp"),
        P(("dp", "tm", "height"), None, None),
        P(),
    )
    return jax.shard_map(
        per_device,
        mesh=mesh,
        in_specs=placed,
        out_specs=(
            P("dp", "tm", "height", None, None),
            P(("dp", "tm", "height"), None, None),
            P(("dp", "tm", "height"), None),
        ),
        check_vma=False,
    )
```

time: 104 us -> 84.1 us (0.81)
  Pallas kernels: 95.8 us -> 78.5 us
  local copies, waits for them, and re-layouts: 5.77 us -> 3.38 us
    pallas_call x1, Pallas kernels: 95.8 us -> 78.5 us  [per_device(): pl.pallas_call(kernel, out_shape=(jax.ShapeDtypeStruct((1024, C), BF16),...]
    unnamed x10 -> x7, local copies, waits for them, and re-layouts: 4.23 us -> 3.38 us
where the time goes in v2:
time: 84.1 us; the launch traced here: 83.9 us
  Pallas kernels  78.5 us (93%)
  local copies, waits for them, and re-layouts  3.38 us (4%)
  between operations  1.94 us (2%)
    pallas_call x1, Pallas kernels, per_device(): pl.pallas_call(kernel, out_shape=(jax.ShapeDtypeStruct((1024, C), BF16),...  78.5 us
    unnamed x7, local copies, waits for them, and re-layouts  3.38 us

profile of v2, /device:TPU:1, one launch (start us, length us, event | category | flops | bytes accessed | tf_op | source)
XLA Modules:
  0.0 83.9 jit_solution(1986540736512227197)
XLA Ops:
  1.9 78.5 %autoencoder_backward.1 = (bf16[1024,384]{1,0:T(8,128)(2,1)}, f32[3,27,384]{2,1,0:T(8,128)}, f32[3,32]{1,0:T(4,128)}) custom-call(s32[1]{0:T(128)S(6)} %copy.17.seeds, s32[1]{0:T(128)S(6)} %copy.18.lengths, bf16[1024,384]{1,0:T(8,128)(2,1)} %bitcast.6, f32[128,128]{1,0:T(8,128)} %bitcast.8, bf16[32,384]{1,0:T(8,128)(2,1)} %bitcast.9, ...), custom_call_target="tpu_custom_call" | custom-call | tf_op jit(solution)/shard_map/autoencoder_backward/pallas_call | solution.py:576
  80.5 0.0 copy-start
  80.5 2.1 %copy.19 = bf16[1,2,8,64,384]{4,3,2,1,0:T(8,128)(2,1)} copy(bf16[1,2,8,64,384]{4,3,2,1,0:T(8,128)(2,1)} %bitcast.5) | data formatting | bytes 1572864
  82.6 0.0 copy-done
  82.6 0.0 copy-start.1
  82.6 0.7 copy.20
  83.3 0.0 copy-done.1
  83.3 0.6 copy.21
Async XLA Ops:
  80.5 2.1 %copy-start = (f32[3,27,384]{2,1,0:T(8,128)S(1)}, f32[3,27,384]{2,1,0:T(8,128)}, u32[]{:S(2)}) copy-start(f32[3,27,384]{2,1,0:T(8,128)} %get-tuple-element.13) | copy-start | bytes 373252
  82.6 0.7 copy-start.1

commit v3 on v2

--- a/solution.py
+++ b/solution.py
@@ -76,9 +76,9 @@
     seeds, lengths, bout, lgrad, hwt, binp, cw, order, swap, fold, pick,
     out_ig, out_cg, out_hg,
     ush, wg, wt, gs, hs, rg, rh, grid, act3, act_t, ao, hin, hpart, hpart_in,
-    sb, r1, p2, r2, p3, r3, fin, fin_in, ybuf, part, part_in,
+    sb, r1, p2, r2, p3, r3, r4, fin, fin_in, ybuf, part, part_in,
     a1_s, a1_r, a2_s, a2_r, a3_s, a3_r, a4_s, a4_r, g_s, g_r, gf_s, gf_r, h_s, h_r, hf_s, hf_r, own_sem,
-    d2d_s, d2d_r, c1_s, c1_r, c2_s, c2_r, c3_s, c3_r,
+    d2d_s, d2d_r, c1_s, c1_r, c2_s, c2_r, c3_s, c3_r, c4_s, c4_r,
 ):
     dp = lax.axis_index("dp")
     tm = lax.axis_index("tm")
@@ -102,8 +102,10 @@
     def halo_peer(step):
         return dev(xh * 2 + 1 - xl, y, lax.rem(z + step, 4), core)
 
-    def across(step):
-        return dev(x, y, lax.rem(z + step, 4), 1 - core)
+    def across(axis, step):
+        place = [x, y, z]
+        place[axis] = lax.rem(place[axis] + step, 4)
+        return dev(*place, 1 - core)
 
     def send(src, dst, s_sem, r_sem, where):
         copy = pltpu.make_async_remote_copy(
@@ -115,7 +117,7 @@
 
     barrier = pltpu.get_barrier_semaphore()
     friends = [peer(axis, step) for axis in range(3) for step in (1, 2, 3)]
-    friends += [across(step) for step in range(4)]
+    friends += [partner] + [across(axis, step) for axis in range(3) for step in (1, 2, 3)]
     friends += [halo_peer(step) for step in (1, 2, 3)]
     for friend in friends:
         pl.semaphore_signal(barrier, inc=1, device_id=friend, device_id_type=MESH)
@@ -202,7 +204,7 @@
     for step in (2, 1, 3):
         ag1.append(send(ush.at[core], here, a1_s.at[step], a1_r.at[step], peer(2, step)))
     for step in (0, 2, 1, 3):
-        ag1.append(send(ush.at[1 - core], here, a1_s.at[4 + step], a1_r.at[4 + step], across(step)))
+        ag1.append(send(ush.at[1 - core], here, a1_s.at[4 + step], a1_r.at[4 + step], across(2, step)))
 
     lax.fori_loop(1, 3, head_block, 0)
     send_frames(1)
@@ -303,10 +305,13 @@
         if g_copy is not None:
             g_copy.wait_recv()
             g_forward.append(send(rg.at[slot], rg.at[slot], gf_s.at[step], gf_r.at[step], partner))
+            if step == 1:
+                relay(1)
+            if step == 2:
+                relay(3)
         h_copy.wait_recv()
         h_forward.append(send(rh.at[slot], rh.at[slot], hf_s.at[step], hf_r.at[step], partner))
-    relay(1)
-    relay(3)
+    relay(2)
     own.wait()
     for copy in g_forward + h_forward:
         copy.wait_recv()
@@ -376,7 +381,6 @@
             copy.start()
 
     tap_pairs(0)
-    relay(2)
     tap_pairs(1)
     pl.when(core == 0)(lambda: single(0))
     start_single(0)
@@ -407,18 +411,26 @@
 
     lax.fori_loop(0, 24, turn_weights, 0, unroll=4)
 
-    weights = wt[...].reshape(3 * C, 5 * C)
+    weights = wt.reshape(3 * C, 5 * C)
 
     def grad_act(owner):
-        cells = []
-        for m in range(5):
-            spot = 4 * core + m
-            i = lax.div(spot, 3)
-            j = lax.rem(spot, 3)
-            cells.append(grid[pl.ds(owner * 2 + 2 - i, 2), pl.ds(2 - j, 8)].reshape(1024, C))
-        ybuf[...] = lax.dot_general(
-            jnp.concatenate(cells, axis=1), weights, NT, preferred_element_type=F32
-        )
+        def of_core(number):
+            cells = []
+            for m in range(5):
+                i, j = divmod(4 * number + m, 3)
+                cells.append(grid[pl.ds(owner * 2 + 2 - i, 2), 2 - j : 10 - j].reshape(1024, C))
+            cells = jnp.concatenate(cells, axis=1)
+            first = slice(0, 5 * C) if number == 0 else slice(C, 5 * C)
+            last = slice(0, 4 * C) if number == 0 else slice(0, 5 * C)
+            ybuf[:, : 2 * C] = lax.dot_general(
+                cells[:, first], weights[: 2 * C, first], NT, preferred_element_type=F32
+            )
+            ybuf[:, 2 * C :] = lax.dot_general(
+                cells[:, last], weights[2 * C :, last], NT, preferred_element_type=F32
+            )
+
+        pl.when(core == 0)(lambda: of_core(0))
+        pl.when(core == 1)(lambda: of_core(1))
 
     def shifted(rows):
         column = lax.broadcasted_iota(jnp.int32, (64, C), 0)
@@ -497,8 +509,16 @@
             rows = [total[n * 24 + a * 6 : n * 24 + a * 6 + 6] for n in range(5)]
             p3[group, a] = jnp.concatenate(rows + [jnp.zeros((2, C), F32)], axis=0).astype(BF16)
         axis = AXES[group][2]
-        for step in (2, 1, 3):
+        for step in (2, 1, 3, 0):
             target = lax.rem(coords[axis] + step, 4)
+            c3.append(
+                send(
+                    p3.at[group, target], r4.at[group, step],
+                    c4_s.at[group, step], c4_r.at[group, step], across(axis, step),
+                )
+            )
+            if step == 0:
+                continue
             c3.append(
                 send(
                     p3.at[group, target], r3.at[group, step - 1],
@@ -532,8 +552,10 @@
         for step in range(3):
             total = total + r3[group, step].astype(F32)
         fin[group] = total
-    last = send(fin, fin_in, d2d_s.at[3], d2d_r.at[3], partner)
-    last.wait_recv()
+        total = r4[group, 0].astype(F32)
+        for step in (1, 2, 3):
+            total = total + r4[group, step].astype(F32)
+        fin_in[group] = total
 
     def result(holder, group, n):
         value = jnp.where(core == holder, fin[group, n * 6 : n * 6 + 6], fin_in[group, n * 6 : n * 6 + 6])
@@ -561,7 +583,7 @@
                 copy.wait_send()
 
         for_user(group, left)
-    for copy in (*ag2.values(), *ag3.values(), *ag4.values(), hp_copy, act_copy, part_copy, last):
+    for copy in (*ag2.values(), *ag3.values(), *ag4.values(), hp_copy, act_copy, part_copy):
         copy.wait_send()
 
 
@@ -603,6 +625,7 @@
             pltpu.VMEM((3, 3, 128, C), BF16),
             pltpu.VMEM((3, 4, 32, C), BF16),
             pltpu.VMEM((3, 3, 32, C), BF16),
+            pltpu.VMEM((3, 4, 32, C), BF16),
             pltpu.VMEM((3, 32, C), F32),
             pltpu.VMEM((3, 32, C), F32),
             pltpu.VMEM((1024, 3 * C), F32),
@@ -617,6 +640,7 @@
             dma((9, 3)), dma((9, 3)),
             dma((3, 3)), dma((3, 3)),
             dma((3, 3)), dma((3, 3)),
+            dma((3, 4)), dma((3, 4)),
         ],
         compiler_params=pltpu.CompilerParams(
             collective_id=0, has_side_effects=True, vmem_limit_bytes=63 * 2**20

time: 84.1 us -> 82.9 us (0.986)
  Pallas kernels: 78.5 us -> 77.4 us
    pallas_call x1, Pallas kernels: 78.5 us -> 77.4 us  [per_device(): pl.pallas_call(kernel, out_shape=(jax.ShapeDtypeStruct((1024, C), BF16),...]
where the time goes in v3:
time: 82.9 us; the launch traced here: 82.7 us
  Pallas kernels  77.4 us (93%)
  local copies, waits for them, and re-layouts  3.38 us (4%)
  between operations  1.94 us (2%)
    pallas_call x1, Pallas kernels, per_device(): pl.pallas_call(kernel, out_shape=(jax.ShapeDtypeStruct((1024, C), BF16),...  77.4 us
    unnamed x7, local copies, waits for them, and re-layouts  3.38 us

profile of v3, /device:TPU:1, one launch (start us, length us, event | category | flops | bytes accessed | tf_op | source)
XLA Modules:
  0.0 82.7 jit_solution(2715818889922866924)
XLA Ops:
  1.9 77.4 %autoencoder_backward.1 = (bf16[1024,384]{1,0:T(8,128)(2,1)}, f32[3,27,384]{2,1,0:T(8,128)}, f32[3,32]{1,0:T(4,128)}) custom-call(s32[1]{0:T(128)S(6)} %copy.17.seeds, s32[1]{0:T(128)S(6)} %copy.18.lengths, bf16[1024,384]{1,0:T(8,128)(2,1)} %bitcast.6, f32[128,128]{1,0:T(8,128)} %bitcast.8, bf16[32,384]{1,0:T(8,128)(2,1)} %bitcast.9, ...), custom_call_target="tpu_custom_call" | custom-call | tf_op jit(solution)/shard_map/autoencoder_backward/pallas_call | solution.py:598
  79.3 0.0 copy-start
  79.3 2.1 %copy.19 = bf16[1,2,8,64,384]{4,3,2,1,0:T(8,128)(2,1)} copy(bf16[1,2,8,64,384]{4,3,2,1,0:T(8,128)(2,1)} %bitcast.5) | data formatting | bytes 1572864
  81.5 0.0 copy-done
  81.5 0.0 copy-start.1
  81.5 0.7 copy.20
  82.1 0.0 copy-done.1
  82.1 0.6 copy.21
Async XLA Ops:
  79.3 2.1 %copy-start = (f32[3,27,384]{2,1,0:T(8,128)S(1)}, f32[3,27,384]{2,1,0:T(8,128)}, u32[]{:S(2)}) copy-start(f32[3,27,384]{2,1,0:T(8,128)} %get-tuple-element.13) | copy-start | bytes 373252
  81.5 0.7 copy-start.1
